TPU v7x, 32 devices: a whole 2x2x4 slice. The times are simulated.
32 devices in a mesh: view: 8 (over z, x), tile: 4 (over y, core).
Axes of the slice: x: 2, y: 2, z: 4, core: 2. Of those that a mesh axis runs over, the one named last changes fastest.
Arguments:
- ref_feat: bfloat16 [32, 8192], P(None, 'tile'), may hold values from -6 to 6
- src_feat: bfloat16 [8, 4, 32, 6144], P('view', 'tile'), may hold values from -6 to 6
- taps: int32 [8, 128, 4], P('view', None, 'tile'), may hold values from 0 to 3838, as said below
- weights: bfloat16 [8, 128, 4, 8192], P('view', None, None, 'tile'), may hold values from 0 to 1, as said below
- conv_weight: float32 [3, 3, 3, 8], replicated, may hold values from -0.4375 to 0.4375
Outputs:
- log_prob: float32 [128, 8192], P('view', 'tile')
- depth_map: float32 [8192], P('tile')
Inputs may be any that keep to these rules, and one draw needn't show every extreme that they name: Every offset keeps all four taps of every pixel of the band inside the band's window. For each view, plane and pixel the four weights are (1 - a)(1 - b), a(1 - b), (1 - a) b, a b for some a, b in 0 to 1, rounded to bfloat16.
All inputs are finite; a program needn't handle non-finite values.
Results may differ from a plain program's by a relative error of at most 0.0003.
Values sent between devices are 32-bit elements; how exact they have to be, the bound alone decides.
A program may use at most 128 MiB of HBM per device.

v0:
```python
import math

import jax
import jax.numpy as jnp
from jax import lax
from jax.sharding import PartitionSpec as P

COLS = 256


def extended_2(shard, sides, width):
    for axis, dim in sides:
        devices, length = (lax.axis_size(axis), shard.shape[dim])
        up = [(i, (i + 1) % devices) for i in range(devices - 1)]
        down = [(j, i) for i, j in up]
        last = lax.slice_in_dim(shard, length - width, length, axis=dim)
        leading = lax.slice_in_dim(shard, 0, width, axis=dim)
        before = lax.ppermute(last, axis, up)
        after = lax.ppermute(leading, axis, down)
        shard = jnp.concatenate([before, shard, after], axis=dim)
    return shard


def correlate_block(window, ref_values, block_offsets, block_weights, group_count, col_count):
    pixel_count = ref_values.shape[1]
    chan_count = ref_values.shape[0]
    span = pixel_count + col_count + 1
    strips = jax.vmap(lambda start: lax.dynamic_slice_in_dim(window, start, span, 1))(block_offsets)
    shifts = (0, 1, col_count, col_count + 1)
    warped = jnp.zeros((block_offsets.shape[0], chan_count, pixel_count), jnp.float32)
    for tap_index in range(4):
        shift = shifts[tap_index]
        cut = strips[:, :, shift : shift + pixel_count].astype(jnp.float32)
        warped = warped + block_weights[:, tap_index].astype(jnp.float32)[:, None, :] * cut
    products = (ref_values[None] * warped).reshape(
        block_offsets.shape[0], group_count, chan_count // group_count, pixel_count
    )
    return jnp.sum(products, axis=2) / (chan_count // group_count)


def stencil(extended, kernel, depth_count, row_count, col_count):
    result = jnp.zeros((depth_count, row_count, col_count), jnp.float32)
    for shift_d in range(3):
        for shift_r in range(3):
            for shift_c in range(3):
                window_cut = extended[
                    shift_d : shift_d + depth_count,
                    :,
                    shift_r : shift_r + row_count,
                    shift_c : shift_c + col_count,
                ]
                result = result + jnp.sum(
                    window_cut * kernel[shift_d, shift_r, shift_c][None, :, None, None], axis=1
                )
    return result


def on_device(ref_feat, src_feat, taps, weights, conv_weight):
    view_count = lax.axis_size("view")
    pixel_count = ref_feat.shape[1]
    depth_count = taps.shape[1]
    slab_size = depth_count // view_count
    group_count = conv_weight.shape[3]
    col_count = COLS
    row_count = pixel_count // col_count
    window = src_feat[0, 0]
    offsets = taps[0, :, 0]
    ref_values = ref_feat.astype(jnp.float32)

    def block_step(block_inputs):
        return correlate_block(
            window, ref_values, block_inputs[0], block_inputs[1], group_count, col_count
        )

    row_total = slab_size * lax.axis_size("view")
    block_size = math.gcd(row_total, 16)
    offset_cut = offsets.reshape(row_total // block_size, block_size)
    weight_cut = weights[0].reshape(row_total // block_size, block_size, 4, pixel_count)
    blocks_out = lax.map(block_step, (offset_cut, weight_cut))
    slab_cost = lax.psum_scatter(
        blocks_out.reshape(row_total, group_count, pixel_count),
        "view",
        scatter_dimension=0,
        tiled=True,
    )
    grid_cost = slab_cost.reshape(slab_size, group_count, row_count, col_count)
    extended = extended_2(grid_cost, (("view", 0), ("tile", 2)), 1)
    extended = jnp.pad(extended, ((0, 0), (0, 0), (0, 0), (1, 1)))
    filtered = stencil(extended, conv_weight, slab_size, row_count, col_count)
    logit_value = 4.0 * jnp.tanh(0.5 * filtered)
    exp_values = jnp.exp(logit_value)
    plane_index = lax.axis_index("view") * slab_size + lax.iota(jnp.int32, slab_size)
    plane_value = plane_index.astype(jnp.float32) / (depth_count - 1)
    exp_total, depth_weighted = lax.psum(
        (jnp.sum(exp_values, axis=0), jnp.sum(exp_values * plane_value[:, None, None], axis=0)),
        "view",
    )
    log_prob = (logit_value - jnp.log(exp_total)[None]).reshape(slab_size, pixel_count)
    depth_map = (depth_weighted / exp_total).reshape(pixel_count)
    return (log_prob, depth_map)


def solution(mesh):
    placed = (
        P(None, "tile"),
        P("view", "tile", None, None),
        P("view", None, "tile"),
        P("view", None, None, "tile"),
        P(),
    )
    return jax.shard_map(
        on_device,
        mesh=mesh,
        in_specs=placed,
        out_specs=(P("view", "tile"), P("tile")),
        check_vma=False,
    )
```

profile of v0, /device:TPU:0, one launch (start us, length us, event | category | flops | bytes accessed | tf_op | source)
XLA Modules:
  0.0 652.3 jit_solution(12992540650520539843)
XLA Ops:
  10.1 420.7 %while.13 = (s32[]{:T(128)}, f32[8,16,8,2048]{3,2,1,0:T(8,128)}, f32[32,2048]{1,0:T(8,128)S(1)}, bf16[8,16,4,2048]{3,2,1,0:T(4,128)(2,1)}, s32[8,16]{1,0:T(8,128...) while((s32[]{:T(128)}, f32[8,16,8,2048]{3,2,1,0:T(8,128)}, ...), condition=%wide.region_2.3_spmd, body=%wide.region_0.2_spmd.sunk | while | flops 13762612 | bytes 31237252 | solution.py:79
  10.1 34.9 %while.14 = (s32[]{:T(128)}, bf16[32,6144]{1,0:T(8,128)(2,1)}, s32[16,2]{0,1:T(2,128)S(1)}, bf16[16,32,2305]{2,1,0:T(8,128)(2,1)S(1)}, s32[]{:T(128)}) while((s32[]{:T(128)}, bf16[32,6144]{1,0:T(8,128)(2,1)}, s32[16,2]{0,1:T(2,128)S(1)}, bf16[16,32,2305]{2,1,0:T(8,128)(2,1)S(1)}, s32[]{:T(128)}) %tuple.98), condition=%wide.while_cond, body=%wide.while_body.sunk | while | flops 2 | bytes 303265 | solution.py:28
  46.3 5.2 add_multiply_fusion.2
  51.5 5.2 reshape.288
  56.7 4.8 reduce_sum.398
  62.7 34.9 %while.14 = (s32[]{:T(128)}, bf16[32,6144]{1,0:T(8,128)(2,1)}, s32[16,2]{0,1:T(2,128)S(1)}, bf16[16,32,2305]{2,1,0:T(8,128)(2,1)S(1)}, s32[]{:T(128)}) while((s32[]{:T(128)}, bf16[32,6144]{1,0:T(8,128)(2,1)}, s32[16,2]{0,1:T(2,128)S(1)}, bf16[16,32,2305]{2,1,0:T(8,128)(2,1)S(1)}, s32[]{:T(128)}) %tuple.98), condition=%wide.while_cond, body=%wide.while_body.sunk | while | flops 2 | bytes 303265 | solution.py:28
  98.9 5.2 add_multiply_fusion.2
  104.1 5.2 reshape.288
  109.3 4.8 reduce_sum.398
  115.3 34.9 %while.14 = (s32[]{:T(128)}, bf16[32,6144]{1,0:T(8,128)(2,1)}, s32[16,2]{0,1:T(2,128)S(1)}, bf16[16,32,2305]{2,1,0:T(8,128)(2,1)S(1)}, s32[]{:T(128)}) while((s32[]{:T(128)}, bf16[32,6144]{1,0:T(8,128)(2,1)}, s32[16,2]{0,1:T(2,128)S(1)}, bf16[16,32,2305]{2,1,0:T(8,128)(2,1)S(1)}, s32[]{:T(128)}) %tuple.98), condition=%wide.while_cond, body=%wide.while_body.sunk | while | flops 2 | bytes 303265 | solution.py:28
  151.5 5.2 add_multiply_fusion.2
  156.7 5.2 reshape.288
  161.9 4.8 reduce_sum.398
  167.9 34.9 %while.14 = (s32[]{:T(128)}, bf16[32,6144]{1,0:T(8,128)(2,1)}, s32[16,2]{0,1:T(2,128)S(1)}, bf16[16,32,2305]{2,1,0:T(8,128)(2,1)S(1)}, s32[]{:T(128)}) while((s32[]{:T(128)}, bf16[32,6144]{1,0:T(8,128)(2,1)}, s32[16,2]{0,1:T(2,128)S(1)}, bf16[16,32,2305]{2,1,0:T(8,128)(2,1)S(1)}, s32[]{:T(128)}) %tuple.98), condition=%wide.while_cond, body=%wide.while_body.sunk | while | flops 2 | bytes 303265 | solution.py:28
  204.1 5.2 add_multiply_fusion.2
  209.3 5.2 reshape.288
  214.5 4.8 reduce_sum.398
  220.4 34.9 %while.14 = (s32[]{:T(128)}, bf16[32,6144]{1,0:T(8,128)(2,1)}, s32[16,2]{0,1:T(2,128)S(1)}, bf16[16,32,2305]{2,1,0:T(8,128)(2,1)S(1)}, s32[]{:T(128)}) while((s32[]{:T(128)}, bf16[32,6144]{1,0:T(8,128)(2,1)}, s32[16,2]{0,1:T(2,128)S(1)}, bf16[16,32,2305]{2,1,0:T(8,128)(2,1)S(1)}, s32[]{:T(128)}) %tuple.98), condition=%wide.while_cond, body=%wide.while_body.sunk | while | flops 2 | bytes 303265 | solution.py:28
  256.7 5.2 add_multiply_fusion.2
  261.9 5.2 reshape.288
  273.0 34.9 %while.14 = (s32[]{:T(128)}, bf16[32,6144]{1,0:T(8,128)(2,1)}, s32[16,2]{0,1:T(2,128)S(1)}, bf16[16,32,2305]{2,1,0:T(8,128)(2,1)S(1)}, s32[]{:T(128)}) while((s32[]{:T(128)}, bf16[32,6144]{1,0:T(8,128)(2,1)}, s32[16,2]{0,1:T(2,128)S(1)}, bf16[16,32,2305]{2,1,0:T(8,128)(2,1)S(1)}, s32[]{:T(128)}) %tuple.98), condition=%wide.while_cond, body=%wide.while_body.sunk | while | flops 2 | bytes 303265 | solution.py:28
  309.2 5.2 add_multiply_fusion.2
  314.4 5.2 reshape.288
  325.6 34.9 %while.14 = (s32[]{:T(128)}, bf16[32,6144]{1,0:T(8,128)(2,1)}, s32[16,2]{0,1:T(2,128)S(1)}, bf16[16,32,2305]{2,1,0:T(8,128)(2,1)S(1)}, s32[]{:T(128)}) while((s32[]{:T(128)}, bf16[32,6144]{1,0:T(8,128)(2,1)}, s32[16,2]{0,1:T(2,128)S(1)}, bf16[16,32,2305]{2,1,0:T(8,128)(2,1)S(1)}, s32[]{:T(128)}) %tuple.98), condition=%wide.while_cond, body=%wide.while_body.sunk | while | flops 2 | bytes 303265 | solution.py:28
  361.8 5.2 add_multiply_fusion.2
  367.1 5.2 reshape.288
  378.2 34.9 %while.14 = (s32[]{:T(128)}, bf16[32,6144]{1,0:T(8,128)(2,1)}, s32[16,2]{0,1:T(2,128)S(1)}, bf16[16,32,2305]{2,1,0:T(8,128)(2,1)S(1)}, s32[]{:T(128)}) while((s32[]{:T(128)}, bf16[32,6144]{1,0:T(8,128)(2,1)}, s32[16,2]{0,1:T(2,128)S(1)}, bf16[16,32,2305]{2,1,0:T(8,128)(2,1)S(1)}, s32[]{:T(128)}) %tuple.98), condition=%wide.while_cond, body=%wide.while_body.sunk | while | flops 2 | bytes 303265 | solution.py:28
  414.4 5.2 add_multiply_fusion.2
  419.7 5.2 reshape.288
  424.9 4.8 reduce_sum.398
  431.5 151.2 %reduce-scatter.2.cloned.1.call-done = f32[16,8,2048]{2,1,0:T(8,128)} async-done(((f32[128,8,2048]{2,1,0:T(8,128)}), f32[16,8,2048]{2,1,0:T(8,128)}) %reduce-scatter.2.cloned.1.call-update) | async-done | bytes 1048592 | tf_op jit(solution)/shard_map/reduce_scatter | solution.py:80
  610.3 33.8 %all-reduce.2 = (f32[8,256]{1,0:T(8,128)S(1)}, f32[8,256]{1,0:T(8,128)S(1)}) all-reduce(f32[8,256]{1,0:T(8,128)S(1)} %reduce_sum.365, f32[8,256]{1,0:T(8,128)S(1)} %reduce_sum.367), channel_id=1, replica_groups=mesh['view'=8,'tile'=4] {'view'}, use_global_device_ids=true, to_apply=%region_32.33 | all-reduce | flops 4096 | bytes 32768 | tf_op jit(solution)/shard_map/psum | solution.py:94
  (496 shorter events, 342.4 us)
Async XLA Ops:
  7.2 575.5 %reduce-scatter.2.cloned.1.call-start = ((), (), s32[]{:S(2)}) async-start(), calls=%async_computation.1 | async-start | bytes 9437184 | tf_op jit(solution)/shard_map/reduce_scatter | solution.py:80
  430.8 0.7 copy-start.1
  582.7 14.3 %copy-start = (f32[16,8,2048]{2,1,0:T(8,128)S(1)}, f32[16,8,2048]{2,1,0:T(8,128)}, u32[]{:S(2)}) copy-start(f32[16,8,2048]{2,1,0:T(8,128)} %reduce-scatter.2.cloned.1.call-done) | copy-start | bytes 3145732
  583.6 6.3 collective-permute-start
  587.0 6.2 collective-permute-start.1
  594.2 3.6 collective-permute-start.2
  595.5 5.0 collective-permute-start.3
Sparse Core Ops, SparseCore 0:
  430.9 151.7 reduce-scatter.1
where the time goes:
time: 658 us; the launch traced here: 652 us
  local copies, waits for them, and re-layouts  332 us (50%)
  waiting for transfers between devices  157 us (24%)
  other arithmetic  105 us (16%)
  blocking collectives  33.8 us (5%)
  between operations  14.3 us (2%)
  starting transfers between devices  7.48 us (1%)
    gather x384, local copies, waits for them, and re-layouts  277 us
    reduce_scatter x1, waiting for transfers between devices, on_device(): lax.psum_scatter(blocks_out.reshape(row_total, group_count, pixel_count),...  151 us
    mul x8, other arithmetic, correlate_block(): ref_values[None] * warped  41.7 us
    reshape x8, local copies, waits for them, and re-layouts, correlate_block(): (ref_values[None] * warped).reshape(block_offsets.shape[0], group_count,...  41.6 us
    reduce_sum x8, other arithmetic, correlate_block(): return jnp.sum(products, axis=2) / (chan_count // group_count)  38.6 us
    psum x1, blocking collectives, on_device(): lax.psum((jnp.sum(exp_values, axis=0), jnp.sum(exp_values * plane_value[:...  33.8 us
  transfers between devices with their start and end apart: 5, of which 3 were waited for; matrix products, arithmetic and copies ran while one was open for 0% of the time, Pallas kernels for 0%

commit v1 on v0

v1 whole, which is shorter than its diff:
```python
import functools

import jax
import jax.numpy as jnp
from jax import lax
from jax.experimental import pallas as pl
from jax.experimental.pallas import tpu as pltpu
from jax.sharding import PartitionSpec as P

COLS = 256
LANES = 128


def split_bf16(x):
    hi = x.astype(jnp.bfloat16)
    lo = (x - hi.astype(jnp.float32)).astype(jnp.bfloat16)
    return hi, lo


def dot32(a, b):
    return lax.dot_general(a, b, (((1,), (0,)), ((), ())), preferred_element_type=jnp.float32)


def load_features(src_ref, ref_ref, stage, win, ref_f, groups):
    chans = ref_ref.shape[0]
    per_group = chans // groups
    for source, scale, target in ((src_ref.at[0, 0], 1.0, win), (ref_ref, 1.0 / per_group, ref_f)):
        for t in range(target.shape[0]):
            cut = source[:, t * LANES : (t + 1) * LANES].astype(jnp.float32)
            stage[t * chans : (t + 1) * chans] = cut * scale
        for t in range(target.shape[0]):
            for c in range(per_group):
                target[t, c * groups : (c + 1) * groups] = stage[
                    pl.ds(t * chans + c, groups, stride=per_group), :
                ]


def correlate_pair(pair, taps_ref, weights_ref, win, ref_f, wbuf, chi, clo, groups):
    tiles = ref_f.shape[0]
    chans = ref_f.shape[1]
    step = COLS // LANES
    lane = lax.broadcasted_iota(jnp.int32, (chans, LANES), 1)
    for k in range(2):
        wbuf[k] = weights_ref[0, 2 * pair + k].astype(jnp.float32)
    planes = []
    for k in range(2):
        offset = taps_ref[2 * pair + k]
        first = offset >> 7
        rest = offset & (LANES - 1)
        planes.append((first, (LANES - rest) & (LANES - 1), LANES - 1 - rest, lane < LANES - rest, lane < LANES - 1 - rest))
    results = []
    for k in range(2):
        first, turn0, turn1, mask0, mask1 = planes[k]
        cuts = []
        before = None
        out = []
        for j in range(tiles + step + 1):
            raw = win[first + j]
            turned = (pltpu.roll(raw, turn0, 1), pltpu.roll(raw, turn1, 1))
            if before is not None:
                cuts.append((jnp.where(mask0, before[0], turned[0]), jnp.where(mask1, before[1], turned[1])))
            before = turned
            i = len(cuts) - 1 - step
            if i >= 0:
                lanes = slice(i * LANES, (i + 1) * LANES)
                taps4 = (cuts[i][0], cuts[i][1], cuts[i + step][0], cuts[i + step][1])
                warped = None
                for tap in range(4):
                    row = jnp.broadcast_to(wbuf[k, tap : tap + 1, lanes], (groups, LANES))
                    row = jnp.concatenate([row] * (chans // groups), axis=0)
                    warped = row * taps4[tap] if warped is None else warped + row * taps4[tap]
                product = warped * ref_f[i]
                total = product[:groups]
                for c in range(1, chans // groups):
                    total = total + product[c * groups : (c + 1) * groups]
                out.append(total)
        results.append(out)
    start = pl.multiple_of((pair + 1) * 2 * groups, 2 * groups)
    for i in range(tiles):
        hi, lo = split_bf16(jnp.concatenate([results[0][i], results[1][i]], axis=0))
        chi[pl.ds(start, 2 * groups), i * LANES : (i + 1) * LANES] = hi
        clo[pl.ds(start, 2 * groups), i * LANES : (i + 1) * LANES] = lo


def filter_slab(slab, size, groups, whi, wlo, chi, clo):
    pixels = chi.shape[1]
    start = pl.multiple_of(slab * size * groups, 2 * groups)
    high = chi[pl.ds(start, (size + 4) * groups), :]
    low = clo[pl.ds(start, (size + 4) * groups), :]
    part = dot32(whi[...], high) + dot32(whi[...], low) + dot32(wlo[...], high)
    zeros = jnp.zeros((size, COLS), jnp.float32)
    width = pixels + 2 * COLS
    col = lax.broadcasted_iota(jnp.int32, (size, width), 1) & (COLS - 1)
    shifted = []
    for e in range(3):
        total = None
        for b in range(3):
            piece = part[(b * 3 + e) * size : (b * 3 + e + 1) * size]
            pads = [zeros] * (2 - b) + [piece] + [zeros] * b
            piece = jnp.concatenate(pads, axis=1)
            total = piece if total is None else total + piece
        shifted.append(total)
    left = jnp.where(col == 0, 0.0, pltpu.roll(shifted[0], 1, 1))
    right = jnp.where(col == COLS - 1, 0.0, pltpu.roll(shifted[2], width - 1, 1))
    return shifted[1] + left + right


def partial_kernel(size, groups, taps_ref, ref_ref, src_ref, weights_ref, filt_ref, out_ref,
                   stage, win, ref_f, wbuf, chi, clo, whi, wlo):
    planes = weights_ref.shape[1]
    load_features(src_ref, ref_ref, stage, win, ref_f, groups)
    high, low = split_bf16(filt_ref[...])
    whi[...] = high
    wlo[...] = low
    edge = jnp.zeros((2 * groups, chi.shape[1]), jnp.bfloat16)
    for buf in (chi, clo):
        buf[: 2 * groups] = edge
        buf[(planes + 2) * groups :] = edge

    def pair_step(pair, _):
        correlate_pair(pair, taps_ref, weights_ref, win, ref_f, wbuf, chi, clo, groups)
        return 0

    lax.fori_loop(0, planes // 2, pair_step, 0)

    def slab_step(slab, _):
        out_ref[pl.ds(pl.multiple_of(slab * size, size), size), :] = filter_slab(
            slab, size, groups, whi, wlo, chi, clo
        )
        return 0

    lax.fori_loop(0, planes // size, slab_step, 0)


def filter_matrix(conv_weight, size):
    groups = conv_weight.shape[3]
    plane_out = lax.broadcasted_iota(jnp.int32, (size, size + 4), 0)
    plane_in = lax.broadcasted_iota(jnp.int32, (size, size + 4), 1)
    total = 0.0
    for a in range(3):
        band = (plane_in == plane_out + 1 + a)[None, None, :, :, None]
        total = total + jnp.where(band, conv_weight[a][:, :, None, None, :], 0.0)
    return total.reshape(9 * size, (size + 4) * groups)


def partial_scratch(chans, window, pixels, planes, groups, size):
    return [
        pltpu.VMEM((window // LANES * chans, LANES), jnp.float32),
        pltpu.VMEM((window // LANES, chans, LANES), jnp.float32),
        pltpu.VMEM((pixels // LANES, chans, LANES), jnp.float32),
        pltpu.VMEM((2, 4, pixels), jnp.float32),
        pltpu.VMEM(((planes + 4) * groups, pixels), jnp.bfloat16),
        pltpu.VMEM(((planes + 4) * groups, pixels), jnp.bfloat16),
        pltpu.VMEM((9 * size, (size + 4) * groups), jnp.bfloat16),
        pltpu.VMEM((9 * size, (size + 4) * groups), jnp.bfloat16),
    ]


def on_device(ref_feat, src_feat, taps, weights, conv_weight):
    view_count = lax.axis_size("view")
    tile_count = lax.axis_size("tile")
    chans, pixels = ref_feat.shape
    planes = taps.shape[1]
    size = planes // view_count
    groups = conv_weight.shape[3]
    window = src_feat.shape[3]
    rows = pixels // COLS
    vmem = pl.BlockSpec(memory_space=pltpu.VMEM)
    part = pl.pallas_call(
        functools.partial(partial_kernel, size, groups),
        out_shape=jax.ShapeDtypeStruct((planes, pixels + 2 * COLS), jnp.float32),
        in_specs=[pl.BlockSpec(memory_space=pltpu.SMEM), vmem, vmem, vmem, vmem],
        out_specs=vmem,
        scratch_shapes=partial_scratch(chans, window, pixels, planes, groups, size),
        compiler_params=pltpu.CompilerParams(vmem_limit_bytes=48 * 1024 * 1024),
    )(taps[0, :, 0], ref_feat, src_feat, weights, filter_matrix(conv_weight, size))
    slab = lax.psum_scatter(part, "view", scatter_dimension=0, tiled=True)
    up = [(i, i + 1) for i in range(tile_count - 1)]
    down = [(j, i) for i, j in up]
    from_above = lax.ppermute(slab[:, pixels + COLS :], "tile", up)
    from_below = lax.ppermute(slab[:, :COLS], "tile", down)
    z = slab[:, COLS : pixels + COLS]
    z = jnp.concatenate(
        [z[:, :COLS] + from_above, z[:, COLS:-COLS], z[:, -COLS:] + from_below], axis=1
    )
    logit = 4.0 * jnp.tanh(0.5 * z)
    exps = jnp.exp(logit)
    plane = lax.axis_index("view") * size + lax.iota(jnp.int32, size)
    value = plane.astype(jnp.float32) / (planes - 1)
    sums = jnp.stack([jnp.sum(exps, axis=0), jnp.sum(exps * value[:, None], axis=0)])
    sums = lax.psum(sums, "view")
    return logit - jnp.log(sums[0])[None], sums[1] / sums[0]


def solution(mesh):
    placed = (
        P(None, "tile"),
        P("view", "tile", None, None),
        P("view", None, "tile"),
        P("view", None, None, "tile"),
        P(),
    )
    return jax.shard_map(
        on_device,
        mesh=mesh,
        in_specs=placed,
        out_specs=(P("view", "tile"), P("tile")),
        check_vma=False,
    )
```

time: 658 us -> 165 us (0.25)
  local copies, waits for them, and re-layouts: 332 us -> 4.55 us
  other arithmetic: 105 us -> 4.56 us
  waiting for transfers between devices: 157 us -> 70.7 us
  Pallas kernels: 0 us -> 33 us
    gather x384 -> x0, local copies, waits for them, and re-layouts: 277 us -> none
    reduce_scatter x1, waiting for transfers between devices: 151 us -> 67.2 us  [on_device(): slab = lax.psum_scatter(part, 'view', scatter_dimension=0, tiled=True)]
    reduce_sum x14 -> x1, other arithmetic: 49.1 us -> 0.09 us  [on_device(): jnp.sum(exps, axis=0)]
    mul x16 -> x0, other arithmetic: 42 us -> none  [the longest x8 41.7 us: correlate_block(): ref_values[None] * warped]
    reshape x8 -> x0, local copies, waits for them, and re-layouts: 41.6 us -> none  [correlate_block(): (ref_values[None] * warped).reshape(block_offsets.shape[0], group_count,...]
    pallas_call x0 -> x1, Pallas kernels: none -> 33 us  [on_device(): pl.pallas_call(functools.partial(partial_kernel, size, groups), out_shape...]
    dynamic_slice x16 -> x0, local copies, waits for them, and re-layouts: 9.64 us -> none  [on_device(): blocks_out = lax.map(block_step, (offset_cut, weight_cut))]
    dynamic_update_slice x8 -> x0, other arithmetic: 8.65 us -> none  [on_device(): blocks_out = lax.map(block_step, (offset_cut, weight_cut))]
  transfers between devices with their start and end apart: 5 -> 3, of which waited for: 3 -> 3; matrix products, arithmetic and copies ran while one was open for 0% -> 1% of each run, Pallas kernels for 0% -> 0%
where the time goes in v1:
time: 165 us
  waiting for transfers between devices  70.7 us (43%)
  blocking collectives  35.1 us (21%)
  Pallas kernels  33 us (20%)
  between operations  14.2 us (9%)
  other arithmetic  4.56 us (3%)
  local copies, waits for them, and re-layouts  4.55 us (3%)
  starting transfers between devices  2.6 us (2%)
    reduce_scatter x1, waiting for transfers between devices, on_device(): slab = lax.psum_scatter(part, 'view', scatter_dimension=0, tiled=True)  67.2 us
    psum x1, blocking collectives, on_device(): sums = lax.psum(sums, 'view')  35.1 us
    pallas_call x1, Pallas kernels, on_device(): pl.pallas_call(functools.partial(partial_kernel, size, groups), out_shape...  33 us
  transfers between devices with their start and end apart: 3, of which 3 were waited for; matrix products, arithmetic and copies ran while one was open for 1% of the time, Pallas kernels for 0%

profile of v1, /device:TPU:0, one launch (start us, length us, event | category | flops | bytes accessed | tf_op | source)
XLA Modules:
  0.0 164.6 jit_solution(9198198816739011932)
XLA Ops:
  7.2 0.0 copy-start.3
  7.2 0.0 copy-start.2
  7.2 0.0 copy-start.1
  7.2 0.0 copy-start
  7.2 0.0 reduce-scatter.2.cloned.1.call-start
  7.3 0.9 slice_bitcast_fusion.2
  8.2 0.1 copy.7
  8.3 0.1 copy.8
  8.4 0.1 copy.9
  8.5 1.7 %select_add_fusion = f32[3,3,16,20,8]{2,1,0,4,3:T(4,128)} fusion(f32[3,3,8]{1,0,2:T(4,128)S(1)} %copy.9, f32[3,3,8]{1,0,2:T(4,128)S(1)} %copy.8, f32[3,3,8]{1,0,2:T(4,128)S(1)} %copy.7, pred[16,20]{0,1:T(8,128)(4,1)S(1)} %get-tuple-element.11, pred[16,20]{0,1:T(8,128)(4,1)S(1)} %get-tuple-element.12, pred[16,20]{0,1:T(8,128)(4,1)S(1)} %iota_compare_fusion.2), kind=kLoop, calls=%fused_computation | loop fusion | flops 115200 | bytes 93984 | tf_op jit(solution)/shard_map/add | solution.py:142
  10.1 1.6 add.62
  11.8 0.1 copy.10.filt_ref
  11.9 0.0 copy-done.3
  11.9 0.0 copy-done.2
  11.9 0.0 copy-done.1
  11.9 0.0 copy-done
  11.9 33.0 %shard_map.68 = f32[128,2560]{1,0:T(8,128)} custom-call(s32[128]{0:T(128)S(1)} %bitcast.13, bf16[32,2048]{1,0:T(8,128)(2,1)S(1)} %copy-done.2, bf16[1,1,32,6144]{3,2,1,0:T(8,128)(2,1)S(1)} %copy-done.1, bf16[1,128,4,2048]{3,2,1,0:T(4,128)(2,1)S(1)} %copy-done, f32[144,160]{1,0:T(8,128)S(1)} %copy.10.filt_ref), custom_call_target="tpu_custom_call" | custom-call | tf_op jit(solution)/shard_map/pallas_call | solution.py:169
  44.9 0.0 reduce-scatter.2.cloned.1.call-update
  44.9 67.2 %reduce-scatter.2.cloned.1.call-done = f32[16,2560]{1,0:T(8,128)} async-done(((f32[128,2560]{1,0:T(8,128)}), f32[16,2560]{1,0:T(8,128)}) %reduce-scatter.2.cloned.1.call-update) | async-done | bytes 163856 | tf_op jit(solution)/shard_map/reduce_scatter | solution.py:177
  112.1 0.7 slice.46
  112.9 1.3 collective-permute-start
  114.1 0.8 collective-permute-done
  115.0 0.7 slice_add_fusion.1
  115.7 1.3 collective-permute-start.1
  117.0 0.9 slice.47
  117.9 2.6 %collective-permute-done.1 = f32[16,256]{1,0:T(8,128)S(1)} collective-permute-done((f32[16,256]{1,0:T(8,128)S(1)}, f32[16,256]{1,0:T(8,128)S(1)}, u32[]{:S(2)}, u32[]{:S(2)}) %collective-permute-start.1) | collective-permute-done | bytes 16416 | tf_op jit(solution)/shard_map/ppermute | solution.py:181
  120.5 0.7 slice_add_fusion
  121.3 0.1 exponential_reduce_fusion
  121.4 35.1 %psum.7 = f32[2,2048]{1,0:T(2,128)S(1)} all-reduce(f32[2,2048]{1,0:T(2,128)S(1)} %pad_maximum_fusion), channel_id=1, replica_groups=mesh['view'=8,'tile'=4] {'view'}, use_global_device_ids=true, to_apply=%region_3.4 | all-reduce | flops 4096 | bytes 32768 | tf_op jit(solution)/shard_map/psum | solution.py:191
  156.5 0.6 slice_divide_fusion
  157.1 0.7 broadcast_subtract_fusion
  (7 shorter events, 0.1 us)
Async XLA Ops:
  7.2 4.7 %copy-start.3 = (s32[1,128,1]{1,2,0:T(1,128)S(1)}, s32[1,128,1]{1,2,0:T(1,128)}, u32[]{:S(2)}) copy-start(s32[1,128,1]{1,2,0:T(1,128)} %param.7) | copy-start | bytes 1540
  7.2 4.7 %copy-start.2 = (bf16[32,2048]{1,0:T(8,128)(2,1)S(1)}, bf16[32,2048]{1,0:T(8,128)(2,1)}, u32[]{:S(2)}) copy-start(bf16[32,2048]{1,0:T(8,128)(2,1)} %ref_ref.1) | copy-start | bytes 393220
  7.2 4.7 %copy-start.1 = (bf16[1,1,32,6144]{3,2,1,0:T(8,128)(2,1)S(1)}, bf16[1,1,32,6144]{3,2,1,0:T(8,128)(2,1)}, u32[]{:S(2)}) copy-start(bf16[1,1,32,6144]{3,2,1,0:T(8,128)(2,1)} %src_ref.1) | copy-start | bytes 1179652
  7.2 4.7 %copy-start = (bf16[1,128,4,2048]{3,2,1,0:T(4,128)(2,1)S(1)}, bf16[1,128,4,2048]{3,2,1,0:T(4,128)(2,1)}, u32[]{:S(2)}) copy-start(bf16[1,128,4,2048]{3,2,1,0:T(4,128)(2,1)} %weights_ref.1) | copy-start | bytes 6291460
  7.2 104.9 %reduce-scatter.2.cloned.1.call-start = ((), (), s32[]{:S(2)}) async-start(), calls=%async_computation.1 | async-start | bytes 1474560 | tf_op jit(solution)/shard_map/reduce_scatter | solution.py:177
  112.9 2.1 %collective-permute-start = (f32[16,256]{1,0:T(8,128)S(1)}, f32[16,256]{1,0:T(8,128)S(1)}, u32[]{:S(2)}, u32[]{:S(2)}) collective-permute-start(f32[16,256]{1,0:T(8,128)S(1)} %slice.46), channel_id=1, source_target_pairs={{0,1},{1,2},{2,3},{4,5},{5,6},{6,7},{8,9},{9,10},{10,11},{12,13},{... | collective-permute-start | bytes 49160 | tf_op jit(solution)/shard_map/ppermute | solution.py:180
  115.7 4.8 %collective-permute-start.1 = (f32[16,256]{1,0:T(8,128)S(1)}, f32[16,256]{1,0:T(8,128)S(1)}, u32[]{:S(2)}, u32[]{:S(2)}) collective-permute-start(f32[16,256]{1,0:T(8,128)S(1)} %get-tuple-element.5), channel_id=1, source_target_pairs={{1,0},{2,1},{3,2},{5,4},{6,5},{7,6},{9,8},{10,9},{11,10},{13,12},{... | collective-permute-start | bytes 49160 | tf_op jit(solution)/shard_map/ppermute | solution.py:181
Sparse Core Ops, SparseCore 0:
  45.1 67.0 reduce-scatter.1

commit v2 on v1

--- a/solution.py
+++ b/solution.py
@@ -9,6 +9,7 @@
 
 COLS = 256
 LANES = 128
+MESH = pl.DeviceIdType.MESH
 
 
 def split_bf16(x):
@@ -105,9 +106,71 @@
     return shifted[1] + left + right
 
 
-def partial_kernel(size, groups, taps_ref, ref_ref, src_ref, weights_ref, filt_ref, out_ref,
-                   stage, win, ref_f, wbuf, chi, clo, whi, wlo):
-    planes = weights_ref.shape[1]
+def peer_at(view, tile):
+    return {"view": view, "tile": tile}
+
+
+def greet_peers(views, tiles, barrier):
+    view, tile = lax.axis_index("view"), lax.axis_index("tile")
+    for k in range(1, views):
+        pl.semaphore_signal(barrier, inc=1, device_id=peer_at(lax.rem(view + k, views), tile), device_id_type=MESH)
+    for k in (1, tiles - 1):
+        pl.semaphore_signal(barrier, inc=1, device_id=peer_at(view, lax.rem(tile + k, tiles)), device_id_type=MESH)
+
+
+def finish(views, tiles, zown, zin, hout, hin, sout, sin, slab_wait, hsend, hrecv, ssend, srecv, prob_ref, depth_ref):
+    view, tile = lax.axis_index("view"), lax.axis_index("tile")
+    size, width = zown.shape
+    total = zown[...]
+    for k in range(views - 1):
+        slab_wait(k)
+        total = total + zin[k]
+    hout[0] = total[:, :COLS]
+    hout[1] = total[:, width - COLS :]
+    halo = []
+    for side, k in ((0, tiles - 1), (1, 1)):
+        halo.append(pltpu.make_async_remote_copy(
+            src_ref=hout.at[side], dst_ref=hin.at[side], send_sem=hsend.at[side], recv_sem=hrecv.at[side],
+            device_id=peer_at(view, lax.rem(tile + k, tiles)), device_id_type=MESH))
+    for copy in halo:
+        copy.start()
+    for copy in halo:
+        copy.wait()
+    below = jnp.where(tile < tiles - 1, hin[0], 0.0)
+    above = jnp.where(tile > 0, hin[1], 0.0)
+    z = total[:, COLS : width - COLS]
+    z = jnp.concatenate([z[:, :COLS] + above, z[:, COLS:-COLS], z[:, -COLS:] + below], axis=1)
+    logit = 4.0 * jnp.tanh(0.5 * z)
+    exps = jnp.exp(logit)
+    plane = view * size + lax.broadcasted_iota(jnp.int32, exps.shape, 0)
+    value = plane.astype(jnp.float32) / (size * views - 1)
+    sout[0:1] = jnp.sum(exps, axis=0, keepdims=True)
+    sout[1:2] = jnp.sum(exps * value, axis=0, keepdims=True)
+    sums = []
+    for k in range(views - 1):
+        sums.append(pltpu.make_async_remote_copy(
+            src_ref=sout, dst_ref=sin.at[k], send_sem=ssend.at[k], recv_sem=srecv.at[k],
+            device_id=peer_at(lax.rem(view + 1 + k, views), tile), device_id_type=MESH))
+    for copy in sums:
+        copy.start()
+    both = sout[...]
+    for k, copy in enumerate(sums):
+        copy.wait_recv()
+        both = both + sin[k]
+    prob_ref[...] = logit - jnp.log(both[0:1])
+    depth_ref[...] = both[1:2] / both[0:1]
+    for copy in sums:
+        copy.wait_send()
+
+
+def slab_copy(views, k, source, zin, zsend, zrecv):
+    view, tile = lax.axis_index("view"), lax.axis_index("tile")
+    return pltpu.make_async_remote_copy(
+        src_ref=source, dst_ref=zin.at[k], send_sem=zsend.at[k], recv_sem=zrecv.at[k],
+        device_id=peer_at(lax.rem(view + 1 + k, views), tile), device_id_type=MESH)
+
+
+def prepare(taps_ref, ref_ref, src_ref, filt_ref, stage, win, ref_f, chi, clo, whi, wlo, groups):
     load_features(src_ref, ref_ref, stage, win, ref_f, groups)
     high, low = split_bf16(filt_ref[...])
     whi[...] = high
@@ -115,21 +178,44 @@
     edge = jnp.zeros((2 * groups, chi.shape[1]), jnp.bfloat16)
     for buf in (chi, clo):
         buf[: 2 * groups] = edge
-        buf[(planes + 2) * groups :] = edge
-
-    def pair_step(pair, _):
+        buf[chi.shape[0] - 2 * groups :] = edge
+
+
+def whole_kernel(size, groups, views, tiles, taps_ref, ref_ref, src_ref, weights_ref, filt_ref, prob_ref, depth_ref,
+                 stage, win, ref_f, wbuf, chi, clo, whi, wlo, zout,
+                 zin, hout, hin, sout, sin, zsend, zrecv, hsend, hrecv, ssend, srecv):
+    barrier = pltpu.get_barrier_semaphore()
+    greet_peers(views, tiles, barrier)
+    prepare(taps_ref, ref_ref, src_ref, filt_ref, stage, win, ref_f, chi, clo, whi, wlo, groups)
+    pl.semaphore_wait(barrier, views + 1)
+    view = lax.axis_index("view")
+    pairs = weights_ref.shape[1] // 2
+    half = size // 2
+
+    def pair_step(q, _):
+        pair = lax.rem(half * (view + 1) - 1 + q, pairs)
         correlate_pair(pair, taps_ref, weights_ref, win, ref_f, wbuf, chi, clo, groups)
         return 0
 
-    lax.fori_loop(0, planes // 2, pair_step, 0)
-
-    def slab_step(slab, _):
-        out_ref[pl.ds(pl.multiple_of(slab * size, size), size), :] = filter_slab(
-            slab, size, groups, whi, wlo, chi, clo
-        )
+    def slab_step(k, _):
+        first = half * k + jnp.where(k > 0, 2, 0)
+        last = half * (k + 1) + jnp.where(k < views - 1, 2, 1)
+        lax.fori_loop(first, last, pair_step, 0)
+        slab = lax.rem(view + 1 + k, views)
+        zout[k] = filter_slab(slab, size, groups, whi, wlo, chi, clo)
+
+        @pl.when(k < views - 1)
+        def _():
+            slab_copy(views, k, zout.at[k], zin, zsend, zrecv).start()
+
         return 0
 
-    lax.fori_loop(0, planes // size, slab_step, 0)
+    lax.fori_loop(0, views, slab_step, 0)
+    copies = [slab_copy(views, k, zout.at[k], zin, zsend, zrecv) for k in range(views - 1)]
+    finish(views, tiles, zout.at[views - 1], zin, hout, hin, sout, sin,
+           lambda k: copies[k].wait_recv(), hsend, hrecv, ssend, srecv, prob_ref, depth_ref)
+    for copy in copies:
+        copy.wait_send()
 
 
 def filter_matrix(conv_weight, size):
@@ -156,40 +242,46 @@
     ]
 
 
+def exchange_scratch(views, size, pixels):
+    width = pixels + 2 * COLS
+    return [
+        pltpu.VMEM((views - 1, size, width), jnp.float32),
+        pltpu.VMEM((2, size, COLS), jnp.float32),
+        pltpu.VMEM((2, size, COLS), jnp.float32),
+        pltpu.VMEM((2, pixels), jnp.float32),
+        pltpu.VMEM((views - 1, 2, pixels), jnp.float32),
+        pltpu.SemaphoreType.DMA((views - 1,)),
+        pltpu.SemaphoreType.DMA((views - 1,)),
+        pltpu.SemaphoreType.DMA((2,)),
+        pltpu.SemaphoreType.DMA((2,)),
+        pltpu.SemaphoreType.DMA((views - 1,)),
+        pltpu.SemaphoreType.DMA((views - 1,)),
+    ]
+
+
 def on_device(ref_feat, src_feat, taps, weights, conv_weight):
-    view_count = lax.axis_size("view")
-    tile_count = lax.axis_size("tile")
+    views = lax.axis_size("view")
+    tiles = lax.axis_size("tile")
     chans, pixels = ref_feat.shape
     planes = taps.shape[1]
-    size = planes // view_count
+    size = planes // views
     groups = conv_weight.shape[3]
     window = src_feat.shape[3]
-    rows = pixels // COLS
+    width = pixels + 2 * COLS
     vmem = pl.BlockSpec(memory_space=pltpu.VMEM)
-    part = pl.pallas_call(
-        functools.partial(partial_kernel, size, groups),
-        out_shape=jax.ShapeDtypeStruct((planes, pixels + 2 * COLS), jnp.float32),
-        in_specs=[pl.BlockSpec(memory_space=pltpu.SMEM), vmem, vmem, vmem, vmem],
-        out_specs=vmem,
-        scratch_shapes=partial_scratch(chans, window, pixels, planes, groups, size),
-        compiler_params=pltpu.CompilerParams(vmem_limit_bytes=48 * 1024 * 1024),
-    )(taps[0, :, 0], ref_feat, src_feat, weights, filter_matrix(conv_weight, size))
-    slab = lax.psum_scatter(part, "view", scatter_dimension=0, tiled=True)
-    up = [(i, i + 1) for i in range(tile_count - 1)]
-    down = [(j, i) for i, j in up]
-    from_above = lax.ppermute(slab[:, pixels + COLS :], "tile", up)
-    from_below = lax.ppermute(slab[:, :COLS], "tile", down)
-    z = slab[:, COLS : pixels + COLS]
-    z = jnp.concatenate(
-        [z[:, :COLS] + from_above, z[:, COLS:-COLS], z[:, -COLS:] + from_below], axis=1
-    )
-    logit = 4.0 * jnp.tanh(0.5 * z)
-    exps = jnp.exp(logit)
-    plane = lax.axis_index("view") * size + lax.iota(jnp.int32, size)
-    value = plane.astype(jnp.float32) / (planes - 1)
-    sums = jnp.stack([jnp.sum(exps, axis=0), jnp.sum(exps * value[:, None], axis=0)])
-    sums = lax.psum(sums, "view")
-    return logit - jnp.log(sums[0])[None], sums[1] / sums[0]
+    inputs = (taps[0, :, 0], ref_feat, src_feat, weights, filter_matrix(conv_weight, size))
+    in_specs = [pl.BlockSpec(memory_space=pltpu.SMEM), vmem, vmem, vmem, vmem]
+    outs = (jax.ShapeDtypeStruct((size, pixels), jnp.float32), jax.ShapeDtypeStruct((1, pixels), jnp.float32))
+    local = partial_scratch(chans, window, pixels, planes, groups, size)
+    log_prob, depth_map = pl.pallas_call(
+        functools.partial(whole_kernel, size, groups, views, tiles),
+        out_shape=outs,
+        in_specs=in_specs,
+        out_specs=(vmem, vmem),
+        scratch_shapes=local + [pltpu.VMEM((views, size, width), jnp.float32)] + exchange_scratch(views, size, pixels),
+        compiler_params=pltpu.CompilerParams(collective_id=0, has_side_effects=True, vmem_limit_bytes=48 * 1024 * 1024),
+    )(*inputs)
+    return log_prob, depth_map[0]
 
 
 def solution(mesh):

time: 165 us -> 59.4 us (0.36)
  waiting for transfers between devices: 70.7 us -> 0 us
  blocking collectives: 35.1 us -> 0 us
  Pallas kernels: 33 us -> 52.2 us
  between operations: 14.2 us -> 0.75 us
  other arithmetic: 4.56 us -> 1.67 us
  starting transfers between devices: 2.6 us -> 0 us
    reduce_scatter x1 -> x0, waiting for transfers between devices: 67.2 us -> none  [on_device(): slab = lax.psum_scatter(part, 'view', scatter_dimension=0, tiled=True)]
    psum x1 -> x0, blocking collectives: 35.1 us -> none  [on_device(): sums = lax.psum(sums, 'view')]
    pallas_call x1, Pallas kernels: 33 us -> 52.2 us  [on_device(): pl.pallas_call(functools.partial(whole_kernel, size, groups, views, tiles...]
    ppermute x2 -> x0, waiting for transfers between devices: 3.45 us -> none  [the longest x1 2.64 us: on_device(): from_below = lax.ppermute(slab[:, :COLS], 'tile', down)]
    ppermute x2 -> x0, starting transfers between devices: 2.56 us -> none  [the longest x1 1.28 us: on_device(): from_below = lax.ppermute(slab[:, :COLS], 'tile', down)]
  transfers between devices with their start and end apart: 3 -> 0, of which waited for: 3 -> 0; matrix products, arithmetic and copies ran while one was open for 1% -> 0% of each run, Pallas kernels for 0% -> 0%
where the time goes in v2:
time: 59.4 us; the launch traced here: 58.8 us
  Pallas kernels  52.2 us (88%)
  local copies, waits for them, and re-layouts  4.19 us (7%)
  other arithmetic  1.67 us (3%)
  between operations  0.75 us (1%)
    pallas_call x1, Pallas kernels, on_device(): pl.pallas_call(functools.partial(whole_kernel, size, groups, views, tiles...  52.2 us
    add x2, local copies, waits for them, and re-layouts, filter_matrix(): total = total + jnp.where(band, conv_weight[a][:, :, None, None, :], 0.0)  1.74 us
    add x1, other arithmetic, filter_matrix(): total = total + jnp.where(band, conv_weight[a][:, :, None, None, :], 0.0)  1.64 us
    unnamed x10, local copies, waits for them, and re-layouts  1.27 us

profile of v2, /device:TPU:0, one launch (start us, length us, event | category | flops | bytes accessed | tf_op | source)
XLA Modules:
  0.0 58.8 jit_solution(10014897488728240098)
XLA Ops:
  0.6 0.0 copy-start
  0.6 0.0 copy-start.3
  0.7 0.0 copy-start.1
  0.7 0.0 copy-start.2
  0.7 0.9 %slice_bitcast_fusion.2 = (f32[3,3,8]{2,1,0:T(4,128)S(1)}, f32[3,3,8]{2,1,0:T(4,128)S(1)}, f32[3,3,8]{2,1,0:T(4,128)S(1)}) fusion(f32[3,3,3,8]{3,2,1,0:T(4,128)} %param.9), kind=kLoop, calls=%fused_computation.6 | loop fusion | bytes 1728 | tf_op jit(solution)/shard_map/jit(_where)/broadcast_in_dim | solution.py:228
  1.6 0.1 copy.7
  1.7 0.1 copy.9
  1.8 0.1 copy.8
  1.9 1.6 %select_add_fusion = f32[3,3,16,20,8]{2,1,0,4,3:T(4,128)} fusion(f32[3,3,8]{1,0,2:T(4,128)S(1)} %copy.9, f32[3,3,8]{1,0,2:T(4,128)S(1)} %copy.8, f32[3,3,8]{1,0,2:T(4,128)S(1)} %copy.7, pred[16,20]{0,1:T(8,128)(4,1)S(1)} %get-tuple-element.9, pred[16,20]{0,1:T(8,128)(4,1)S(1)} %get-tuple-element.10, pred[16,20]{0,1:T(8,128)(4,1)S(1)} %iota_compare_fusion.2), kind=kLoop, calls=%fused_computation | loop fusion | flops 115200 | bytes 93984 | tf_op jit(solution)/shard_map/add | solution.py:228
  3.6 1.6 %add.42 = f32[144,160]{0,1:T(8,128)S(1)} reshape(f32[3,3,16,20,8]{2,1,0,4,3:T(4,128)} %select_add_fusion) | data formatting | bytes 184320 | tf_op jit(solution)/shard_map/add | solution.py:228
  5.2 0.1 copy.10.filt_ref
  5.3 0.0 copy-done
  5.3 0.0 copy-done.3
  5.3 0.0 copy-done.1
  5.3 0.0 copy-done.2
  5.3 52.2 %shard_map.68 = (f32[16,2048]{1,0:T(8,128)S(1)}, f32[1,2048]{1,0:T(1,128)S(1)}) custom-call(s32[128]{0:T(128)S(1)} %bitcast.11, bf16[32,2048]{1,0:T(8,128)(2,1)S(1)} %copy-done.2, bf16[1,1,32,6144]{3,2,1,0:T(8,128)(2,1)S(1)} %copy-done.1, bf16[1,128,4,2048]{3,2,1,0:T(4,128)(2,1)S(1)} %copy-done, f32[144,160]{1,0:T(8,128)S(1)} %copy.10.filt_ref), custom_call_target="tpu_custom_call" | custom-call | tf_op jit(solution)/shard_map/pallas_call | solution.py:276
  57.5 0.7 %copy.13 = f32[16,2048]{1,0:T(8,128)} copy(f32[16,2048]{1,0:T(8,128)S(1)} %get-tuple-element.13) | data formatting | bytes 262144
  58.2 0.6 %copy.14 = f32[2048]{0:T(1024)} copy(f32[2048]{0:T(1024)S(1)} %bitcast.10) | data formatting | bytes 16384
  (5 shorter events, 0.0 us)
Async XLA Ops:
  0.6 4.7 %copy-start = (bf16[1,128,4,2048]{3,2,1,0:T(4,128)(2,1)S(1)}, bf16[1,128,4,2048]{3,2,1,0:T(4,128)(2,1)}, u32[]{:S(2)}) copy-start(bf16[1,128,4,2048]{3,2,1,0:T(4,128)(2,1)} %weights_ref.1) | copy-start | bytes 6291460
  0.6 4.7 %copy-start.3 = (s32[1,128,1]{1,2,0:T(1,128)S(1)}, s32[1,128,1]{1,2,0:T(1,128)}, u32[]{:S(2)}) copy-start(s32[1,128,1]{1,2,0:T(1,128)} %param.7) | copy-start | bytes 1540
  0.7 4.7 %copy-start.1 = (bf16[1,1,32,6144]{3,2,1,0:T(8,128)(2,1)S(1)}, bf16[1,1,32,6144]{3,2,1,0:T(8,128)(2,1)}, u32[]{:S(2)}) copy-start(bf16[1,1,32,6144]{3,2,1,0:T(8,128)(2,1)} %src_ref.1) | copy-start | bytes 1179652
  0.7 4.7 %copy-start.2 = (bf16[32,2048]{1,0:T(8,128)(2,1)S(1)}, bf16[32,2048]{1,0:T(8,128)(2,1)}, u32[]{:S(2)}) copy-start(bf16[32,2048]{1,0:T(8,128)(2,1)} %ref_ref.1) | copy-start | bytes 393220

commit v3 on v2

--- a/solution.py
+++ b/solution.py
@@ -22,59 +22,61 @@
     return lax.dot_general(a, b, (((1,), (0,)), ((), ())), preferred_element_type=jnp.float32)
 
 
-def load_features(src_ref, ref_ref, stage, win, ref_f, groups):
+def load_features(src_ref, ref_ref, stage, win, ref_f, shift, groups):
     chans = ref_ref.shape[0]
     per_group = chans // groups
-    for source, scale, target in ((src_ref.at[0, 0], 1.0, win), (ref_ref, 1.0 / per_group, ref_f)):
-        for t in range(target.shape[0]):
-            cut = source[:, t * LANES : (t + 1) * LANES].astype(jnp.float32)
-            stage[t * chans : (t + 1) * chans] = cut * scale
-        for t in range(target.shape[0]):
-            for c in range(per_group):
-                target[t, c * groups : (c + 1) * groups] = stage[
-                    pl.ds(t * chans + c, groups, stride=per_group), :
-                ]
-
-
-def correlate_pair(pair, taps_ref, weights_ref, win, ref_f, wbuf, chi, clo, groups):
-    tiles = ref_f.shape[0]
-    chans = ref_f.shape[1]
+
+    def ordered(source, scale, t):
+        cut = source[:, t * LANES : (t + 1) * LANES].astype(jnp.float32)
+        stage[t * chans : (t + 1) * chans] = cut * scale
+        return jnp.concatenate(
+            [stage[pl.ds(t * chans + c, groups, stride=per_group), :] for c in range(per_group)], axis=0
+        )
+
+    for t in range(win.shape[0] + 1):
+        tile = ordered(src_ref.at[0, 0], 1.0, t).astype(jnp.bfloat16)
+        if t < win.shape[0]:
+            win[t, :, :LANES] = tile
+        if t > 0:
+            win[t - 1, :, LANES:] = tile
+    for t in range(ref_f.shape[0]):
+        ref_f[t] = ordered(ref_ref, 1.0 / per_group, t)
+    row = lax.broadcasted_iota(jnp.int32, shift.shape, 0)
+    col = lax.broadcasted_iota(jnp.int32, shift.shape, 1)
+    apart = row - jnp.where(col < LANES, col, col - (LANES - 1))
+    shift[...] = apart.astype(jnp.float32).astype(jnp.bfloat16)
+
+
+def correlate_pair(pair, taps_ref, weights_ref, win, ref_f, shift, wbuf, chi, clo, groups):
+    tiles, chans = ref_f.shape[:2]
     step = COLS // LANES
-    lane = lax.broadcasted_iota(jnp.int32, (chans, LANES), 1)
     for k in range(2):
         wbuf[k] = weights_ref[0, 2 * pair + k].astype(jnp.float32)
-    planes = []
+    moved = []
     for k in range(2):
         offset = taps_ref[2 * pair + k]
-        first = offset >> 7
-        rest = offset & (LANES - 1)
-        planes.append((first, (LANES - rest) & (LANES - 1), LANES - 1 - rest, lane < LANES - rest, lane < LANES - 1 - rest))
+        rest = jnp.full((1, 2 * LANES), offset & (LANES - 1), jnp.int32).astype(jnp.float32).astype(jnp.bfloat16)
+        pick = jnp.where(shift[...] == rest, jnp.bfloat16(1), jnp.bfloat16(0))
+        cut = win[pl.ds(offset >> 7, tiles + step)].reshape((tiles + step) * chans, 2 * LANES)
+        moved.append(dot32(cut, pick))
     results = []
     for k in range(2):
-        first, turn0, turn1, mask0, mask1 = planes[k]
-        cuts = []
-        before = None
         out = []
-        for j in range(tiles + step + 1):
-            raw = win[first + j]
-            turned = (pltpu.roll(raw, turn0, 1), pltpu.roll(raw, turn1, 1))
-            if before is not None:
-                cuts.append((jnp.where(mask0, before[0], turned[0]), jnp.where(mask1, before[1], turned[1])))
-            before = turned
-            i = len(cuts) - 1 - step
-            if i >= 0:
-                lanes = slice(i * LANES, (i + 1) * LANES)
-                taps4 = (cuts[i][0], cuts[i][1], cuts[i + step][0], cuts[i + step][1])
-                warped = None
-                for tap in range(4):
-                    row = jnp.broadcast_to(wbuf[k, tap : tap + 1, lanes], (groups, LANES))
-                    row = jnp.concatenate([row] * (chans // groups), axis=0)
-                    warped = row * taps4[tap] if warped is None else warped + row * taps4[tap]
-                product = warped * ref_f[i]
-                total = product[:groups]
-                for c in range(1, chans // groups):
-                    total = total + product[c * groups : (c + 1) * groups]
-                out.append(total)
+        for i in range(tiles):
+            lanes = slice(i * LANES, (i + 1) * LANES)
+            near = moved[k][i * chans : (i + 1) * chans]
+            far = moved[k][(i + step) * chans : (i + step + 1) * chans]
+            taps4 = (near[:, :LANES], near[:, LANES:], far[:, :LANES], far[:, LANES:])
+            warped = None
+            for tap in range(4):
+                row = jnp.broadcast_to(wbuf[k, tap : tap + 1, lanes], (groups, LANES))
+                row = jnp.concatenate([row] * (chans // groups), axis=0)
+                warped = row * taps4[tap] if warped is None else warped + row * taps4[tap]
+            product = warped * ref_f[i]
+            total = product[:groups]
+            for c in range(1, chans // groups):
+                total = total + product[c * groups : (c + 1) * groups]
+            out.append(total)
         results.append(out)
     start = pl.multiple_of((pair + 1) * 2 * groups, 2 * groups)
     for i in range(tiles):
@@ -104,6 +106,25 @@
     left = jnp.where(col == 0, 0.0, pltpu.roll(shifted[0], 1, 1))
     right = jnp.where(col == COLS - 1, 0.0, pltpu.roll(shifted[2], width - 1, 1))
     return shifted[1] + left + right
+
+
+def filter_matrix(filt_ref, whi, wlo, groups):
+    cols = whi.shape[1]
+    size = whi.shape[0] // 9
+    group = lax.broadcasted_iota(jnp.int32, (groups, cols), 0)
+    spread = ((lax.broadcasted_iota(jnp.int32, (groups, cols), 1) & (groups - 1)) == group)
+    spread = spread.astype(jnp.float32).astype(jnp.bfloat16)
+    plane_in = lax.broadcasted_iota(jnp.int32, (size, cols), 1) // groups
+    apart = plane_in - lax.broadcasted_iota(jnp.int32, (size, cols), 0)
+    for b in range(3):
+        over = [[dot32(part, spread) for part in split_bf16(filt_ref[a, b])] for a in range(3)]
+        for e in range(3):
+            at = (b * 3 + e) * size
+            for out, which in ((whi, 0), (wlo, 1)):
+                total = jnp.zeros((size, cols), jnp.float32)
+                for a in range(3):
+                    total = jnp.where(apart == a + 1, over[a][which][e : e + 1], total)
+                out[at : at + size] = total.astype(jnp.bfloat16)
 
 
 def peer_at(view, tile):
@@ -170,11 +191,9 @@
         device_id=peer_at(lax.rem(view + 1 + k, views), tile), device_id_type=MESH)
 
 
-def prepare(taps_ref, ref_ref, src_ref, filt_ref, stage, win, ref_f, chi, clo, whi, wlo, groups):
-    load_features(src_ref, ref_ref, stage, win, ref_f, groups)
-    high, low = split_bf16(filt_ref[...])
-    whi[...] = high
-    wlo[...] = low
+def prepare(taps_ref, ref_ref, src_ref, filt_ref, stage, win, ref_f, shift, chi, clo, whi, wlo, groups):
+    load_features(src_ref, ref_ref, stage, win, ref_f, shift, groups)
+    filter_matrix(filt_ref, whi, wlo, groups)
     edge = jnp.zeros((2 * groups, chi.shape[1]), jnp.bfloat16)
     for buf in (chi, clo):
         buf[: 2 * groups] = edge
@@ -182,11 +201,11 @@
 
 
 def whole_kernel(size, groups, views, tiles, taps_ref, ref_ref, src_ref, weights_ref, filt_ref, prob_ref, depth_ref,
-                 stage, win, ref_f, wbuf, chi, clo, whi, wlo, zout,
+                 stage, win, ref_f, shift, wbuf, chi, clo, whi, wlo, zout,
                  zin, hout, hin, sout, sin, zsend, zrecv, hsend, hrecv, ssend, srecv):
     barrier = pltpu.get_barrier_semaphore()
     greet_peers(views, tiles, barrier)
-    prepare(taps_ref, ref_ref, src_ref, filt_ref, stage, win, ref_f, chi, clo, whi, wlo, groups)
+    prepare(taps_ref, ref_ref, src_ref, filt_ref, stage, win, ref_f, shift, chi, clo, whi, wlo, groups)
     pl.semaphore_wait(barrier, views + 1)
     view = lax.axis_index("view")
     pairs = weights_ref.shape[1] // 2
@@ -194,7 +213,7 @@
 
     def pair_step(q, _):
         pair = lax.rem(half * (view + 1) - 1 + q, pairs)
-        correlate_pair(pair, taps_ref, weights_ref, win, ref_f, wbuf, chi, clo, groups)
+        correlate_pair(pair, taps_ref, weights_ref, win, ref_f, shift, wbuf, chi, clo, groups)
         return 0
 
     def slab_step(k, _):
@@ -218,22 +237,12 @@
         copy.wait_send()
 
 
-def filter_matrix(conv_weight, size):
-    groups = conv_weight.shape[3]
-    plane_out = lax.broadcasted_iota(jnp.int32, (size, size + 4), 0)
-    plane_in = lax.broadcasted_iota(jnp.int32, (size, size + 4), 1)
-    total = 0.0
-    for a in range(3):
-        band = (plane_in == plane_out + 1 + a)[None, None, :, :, None]
-        total = total + jnp.where(band, conv_weight[a][:, :, None, None, :], 0.0)
-    return total.reshape(9 * size, (size + 4) * groups)
-
-
 def partial_scratch(chans, window, pixels, planes, groups, size):
     return [
         pltpu.VMEM((window // LANES * chans, LANES), jnp.float32),
-        pltpu.VMEM((window // LANES, chans, LANES), jnp.float32),
+        pltpu.VMEM((window // LANES - 1, chans, 2 * LANES), jnp.bfloat16),
         pltpu.VMEM((pixels // LANES, chans, LANES), jnp.float32),
+        pltpu.VMEM((2 * LANES, 2 * LANES), jnp.bfloat16),
         pltpu.VMEM((2, 4, pixels), jnp.float32),
         pltpu.VMEM(((planes + 4) * groups, pixels), jnp.bfloat16),
         pltpu.VMEM(((planes + 4) * groups, pixels), jnp.bfloat16),
@@ -269,7 +278,7 @@
     window = src_feat.shape[3]
     width = pixels + 2 * COLS
     vmem = pl.BlockSpec(memory_space=pltpu.VMEM)
-    inputs = (taps[0, :, 0], ref_feat, src_feat, weights, filter_matrix(conv_weight, size))
+    inputs = (taps.reshape(planes), ref_feat, src_feat, weights, conv_weight)
     in_specs = [pl.BlockSpec(memory_space=pltpu.SMEM), vmem, vmem, vmem, vmem]
     outs = (jax.ShapeDtypeStruct((size, pixels), jnp.float32), jax.ShapeDtypeStruct((1, pixels), jnp.float32))
     local = partial_scratch(chans, window, pixels, planes, groups, size)

time: 59.4 us -> 58.6 us (0.987)
  local copies, waits for them, and re-layouts: 4.19 us -> 6.12 us
  other arithmetic: 1.67 us -> 0 us
  Pallas kernels: 52.2 us -> 51 us
    unnamed x10 -> x12, local copies, waits for them, and re-layouts: 1.27 us -> 6.12 us
    add x2 -> x0, local copies, waits for them, and re-layouts: 1.74 us -> none  [filter_matrix(): total = total + jnp.where(band, conv_weight[a][:, :, None, None, :], 0.0)]
    add x4 -> x0, other arithmetic: 1.65 us -> none  [the longest x1 1.64 us: filter_matrix(): total = total + jnp.where(band, conv_weight[a][:, :, None, None, :], 0.0)]
    broadcast_in_dim x4 -> x0, local copies, waits for them, and re-layouts: 1.18 us -> none  [filter_matrix(): total = total + jnp.where(band, conv_weight[a][:, :, None, None, :], 0.0)]
    pallas_call x1, Pallas kernels: 52.2 us -> 51 us  [on_device(): pl.pallas_call(functools.partial(whole_kernel, size, groups, views, tiles...]
where the time goes in v3:
time: 58.6 us; the launch traced here: 57.8 us
  Pallas kernels  51 us (87%)
  local copies, waits for them, and re-layouts  6.12 us (10%)
  between operations  0.65 us (1%)
    pallas_call x1, Pallas kernels, on_device(): pl.pallas_call(functools.partial(whole_kernel, size, groups, views, tiles...  51 us
    unnamed x12, local copies, waits for them, and re-layouts  6.12 us

profile of v3, /device:TPU:0, one launch (start us, length us, event | category | flops | bytes accessed | tf_op | source)
XLA Modules:
  0.0 57.8 jit_solution(3408389084281209238)
XLA Ops:
  0.6 0.0 copy-start
  0.6 1.6 %copy-done = bf16[1,128,4,2048]{3,2,1,0:T(4,128)(2,1)S(1)} copy-done((bf16[1,128,4,2048]{3,2,1,0:T(4,128)(2,1)S(1)}, bf16[1,128,4,2048]{3,2,1,0:T(4,128)(2,1)}, u32[]{:S(2)}) %copy-start) | copy-done | bytes 2097176
  2.2 0.0 copy-start.1
  2.2 1.0 %copy-done.1 = bf16[1,1,32,6144]{3,2,1,0:T(8,128)(2,1)S(1)} copy-done((bf16[1,1,32,6144]{3,2,1,0:T(8,128)(2,1)S(1)}, bf16[1,1,32,6144]{3,2,1,0:T(8,128)(2,1)}, u32[]{:S(2)}) %copy-start.1) | copy-done | bytes 393240
  3.2 0.0 copy-start.2
  3.2 0.9 %copy-done.2 = bf16[32,2048]{1,0:T(8,128)(2,1)S(1)} copy-done((bf16[32,2048]{1,0:T(8,128)(2,1)S(1)}, bf16[32,2048]{1,0:T(8,128)(2,1)}, u32[]{:S(2)}) %copy-start.2) | copy-done | bytes 131096
  4.1 0.0 copy-start.3
  4.1 0.7 %copy-done.3 = f32[3,3,3,8]{3,2,1,0:T(4,128)S(1)} copy-done((f32[3,3,3,8]{3,2,1,0:T(4,128)S(1)}, f32[3,3,3,8]{3,2,1,0:T(4,128)}, u32[]{:S(2)}) %copy-start.3) | copy-done | bytes 888
  4.8 0.0 copy-start.4
  4.8 0.7 %copy-done.4 = s32[1,128,1]{1,2,0:T(1,128)S(1)} copy-done((s32[1,128,1]{1,2,0:T(1,128)S(1)}, s32[1,128,1]{1,2,0:T(1,128)}, u32[]{:S(2)}) %copy-start.4) | copy-done | bytes 536
  5.5 51.0 %shard_map.68 = (f32[16,2048]{1,0:T(8,128)S(1)}, f32[1,2048]{1,0:T(1,128)S(1)}) custom-call(s32[128]{0:T(128)S(1)} %bitcast.3, bf16[32,2048]{1,0:T(8,128)(2,1)S(1)} %copy-done.2, bf16[1,1,32,6144]{3,2,1,0:T(8,128)(2,1)S(1)} %copy-done.1, bf16[1,128,4,2048]{3,2,1,0:T(4,128)(2,1)S(1)} %copy-done, f32[3,3,3,8]{3,2,1,0:T(4,128)S(1)} %copy-done.3), custom_call_target="tpu_custom_call" | custom-call | tf_op jit(solution)/shard_map/pallas_call | solution.py:285
  56.6 0.7 %copy.9 = f32[16,2048]{1,0:T(8,128)} copy(f32[16,2048]{1,0:T(8,128)S(1)} %get-tuple-element.8) | data formatting | bytes 262144
  57.2 0.6 %copy.10 = f32[2048]{0:T(1024)} copy(f32[2048]{0:T(1024)S(1)} %bitcast.2) | data formatting | bytes 16384
Async XLA Ops:
  0.6 1.6 %copy-start = (bf16[1,128,4,2048]{3,2,1,0:T(4,128)(2,1)S(1)}, bf16[1,128,4,2048]{3,2,1,0:T(4,128)(2,1)}, u32[]{:S(2)}) copy-start(bf16[1,128,4,2048]{3,2,1,0:T(4,128)(2,1)} %weights_ref.1) | copy-start | bytes 6291460
  2.2 1.0 %copy-start.1 = (bf16[1,1,32,6144]{3,2,1,0:T(8,128)(2,1)S(1)}, bf16[1,1,32,6144]{3,2,1,0:T(8,128)(2,1)}, u32[]{:S(2)}) copy-start(bf16[1,1,32,6144]{3,2,1,0:T(8,128)(2,1)} %src_ref.1) | copy-start | bytes 1179652
  3.2 0.9 %copy-start.2 = (bf16[32,2048]{1,0:T(8,128)(2,1)S(1)}, bf16[32,2048]{1,0:T(8,128)(2,1)}, u32[]{:S(2)}) copy-start(bf16[32,2048]{1,0:T(8,128)(2,1)} %ref_ref.1) | copy-start | bytes 393220
  4.1 0.7 %copy-start.3 = (f32[3,3,3,8]{3,2,1,0:T(4,128)S(1)}, f32[3,3,3,8]{3,2,1,0:T(4,128)}, u32[]{:S(2)}) copy-start(f32[3,3,3,8]{3,2,1,0:T(4,128)} %filt_ref.1) | copy-start | bytes 2596
  4.8 0.7 %copy-start.4 = (s32[1,128,1]{1,2,0:T(1,128)S(1)}, s32[1,128,1]{1,2,0:T(1,128)}, u32[]{:S(2)}) copy-start(s32[1,128,1]{1,2,0:T(1,128)} %param.7) | copy-start | bytes 1540

commit v4 on v3

--- a/solution.py
+++ b/solution.py
@@ -139,13 +139,9 @@
         pl.semaphore_signal(barrier, inc=1, device_id=peer_at(view, lax.rem(tile + k, tiles)), device_id_type=MESH)
 
 
-def finish(views, tiles, zown, zin, hout, hin, sout, sin, slab_wait, hsend, hrecv, ssend, srecv, prob_ref, depth_ref):
+def finish(views, tiles, total, hout, hin, sout, sin, hsend, hrecv, ssend, srecv, prob_ref, depth_ref):
     view, tile = lax.axis_index("view"), lax.axis_index("tile")
-    size, width = zown.shape
-    total = zown[...]
-    for k in range(views - 1):
-        slab_wait(k)
-        total = total + zin[k]
+    size, width = total.shape
     hout[0] = total[:, :COLS]
     hout[1] = total[:, width - COLS :]
     halo = []
@@ -184,11 +180,18 @@
         copy.wait_send()
 
 
-def slab_copy(views, k, source, zin, zsend, zrecv):
+def side_copy(i, zside, xin, xsend, xrecv):
     view, tile = lax.axis_index("view"), lax.axis_index("tile")
     return pltpu.make_async_remote_copy(
-        src_ref=source, dst_ref=zin.at[k], send_sem=zsend.at[k], recv_sem=zrecv.at[k],
-        device_id=peer_at(lax.rem(view + 1 + k, views), tile), device_id_type=MESH)
+        src_ref=zside.at[i], dst_ref=xin.at[i], send_sem=xsend.at[i], recv_sem=xrecv.at[i],
+        device_id=peer_at(view + 1 - 2 * lax.rem(view, 2), tile), device_id_type=MESH)
+
+
+def owner_copy(views, i, zown, zin, zsend, zrecv):
+    view, tile = lax.axis_index("view"), lax.axis_index("tile")
+    return pltpu.make_async_remote_copy(
+        src_ref=zown.at[i], dst_ref=zin.at[i], send_sem=zsend.at[i], recv_sem=zrecv.at[i],
+        device_id=peer_at(lax.rem(view + 2 + 2 * i, views), tile), device_id_type=MESH)
 
 
 def prepare(taps_ref, ref_ref, src_ref, filt_ref, stage, win, ref_f, shift, chi, clo, whi, wlo, groups):
@@ -200,41 +203,74 @@
         buf[chi.shape[0] - 2 * groups :] = edge
 
 
-def whole_kernel(size, groups, views, tiles, taps_ref, ref_ref, src_ref, weights_ref, filt_ref, prob_ref, depth_ref,
-                 stage, win, ref_f, shift, wbuf, chi, clo, whi, wlo, zout,
-                 zin, hout, hin, sout, sin, zsend, zrecv, hsend, hrecv, ssend, srecv):
+def whole_kernel(size, groups, views, tiles, taps_ref, ref_hbm, src_hbm, weights_hbm, filt_ref, prob_ref, depth_ref,
+                 ref_ref, src_ref, weights_ref, load_sem,
+                 stage, win, ref_f, shift, wbuf, chi, clo, whi, wlo, zside, zown,
+                 xin, zin, hout, hin, sout, sin, xsend, xrecv, zsend, zrecv, hsend, hrecv, ssend, srecv):
+    loads = [
+        pltpu.make_async_copy(source, target, load_sem.at[n])
+        for n, (source, target) in enumerate(
+            ((src_hbm, src_ref), (ref_hbm, ref_ref), (weights_hbm, weights_ref)))
+    ]
+    for load in loads:
+        load.start()
     barrier = pltpu.get_barrier_semaphore()
     greet_peers(views, tiles, barrier)
+    loads[0].wait()
+    loads[1].wait()
     prepare(taps_ref, ref_ref, src_ref, filt_ref, stage, win, ref_f, shift, chi, clo, whi, wlo, groups)
+    loads[2].wait()
     pl.semaphore_wait(barrier, views + 1)
     view = lax.axis_index("view")
-    pairs = weights_ref.shape[1] // 2
+    col = lax.rem(view, 2)
+    rows = views // 2
     half = size // 2
-
-    def pair_step(q, _):
-        pair = lax.rem(half * (view + 1) - 1 + q, pairs)
-        correlate_pair(pair, taps_ref, weights_ref, win, ref_f, shift, wbuf, chi, clo, groups)
+    pairs = half * views
+
+    def pairs_from(origin, first, last):
+        def pair_step(q, _):
+            pair = lax.rem(origin + q + (pairs - 1), pairs)
+            correlate_pair(pair, taps_ref, weights_ref, win, ref_f, shift, wbuf, chi, clo, groups)
+            return 0
+
+        lax.fori_loop(first, last, pair_step, 0)
+
+    def row_step(i, _):
+        row = lax.rem(view // 2 + 1 + i, rows)
+        origin = row * size
+        final = jnp.where(i < rows - 1, 1, 0)
+        low, high = jnp.where(col == 0, half, 2), jnp.where(col == 0, size + final + 1, half + 2)
+
+        @pl.when(i == 0)
+        def _():
+            pairs_from(origin, 0, 2)
+
+        pairs_from(origin, low, high)
+        zside[i] = filter_slab(2 * row + 1 - col, size, groups, whi, wlo, chi, clo)
+        side_copy(i, zside, xin, xsend, xrecv).start()
+        low, high = jnp.where(col == 0, 2, half + 2), jnp.where(col == 0, half, size + final + 1)
+        pairs_from(origin, low, high)
+        own = filter_slab(2 * row + col, size, groups, whi, wlo, chi, clo)
+        side_copy(i, zside, xin, xsend, xrecv).wait_recv()
+        zown[i] = own + xin[i]
+
+        @pl.when(i < rows - 1)
+        def _():
+            owner_copy(views, i, zown, zin, zsend, zrecv).start()
+
         return 0
 
-    def slab_step(k, _):
-        first = half * k + jnp.where(k > 0, 2, 0)
-        last = half * (k + 1) + jnp.where(k < views - 1, 2, 1)
-        lax.fori_loop(first, last, pair_step, 0)
-        slab = lax.rem(view + 1 + k, views)
-        zout[k] = filter_slab(slab, size, groups, whi, wlo, chi, clo)
-
-        @pl.when(k < views - 1)
-        def _():
-            slab_copy(views, k, zout.at[k], zin, zsend, zrecv).start()
-
-        return 0
-
-    lax.fori_loop(0, views, slab_step, 0)
-    copies = [slab_copy(views, k, zout.at[k], zin, zsend, zrecv) for k in range(views - 1)]
-    finish(views, tiles, zout.at[views - 1], zin, hout, hin, sout, sin,
-           lambda k: copies[k].wait_recv(), hsend, hrecv, ssend, srecv, prob_ref, depth_ref)
+    lax.fori_loop(0, rows, row_step, 0)
+    total = zown[rows - 1]
+    copies = [owner_copy(views, i, zown, zin, zsend, zrecv) for i in range(rows - 1)]
+    for i, copy in enumerate(copies):
+        copy.wait_recv()
+        total = total + zin[i]
+    finish(views, tiles, total, hout, hin, sout, sin, hsend, hrecv, ssend, srecv, prob_ref, depth_ref)
     for copy in copies:
         copy.wait_send()
+    for i in range(rows):
+        side_copy(i, zside, xin, xsend, xrecv).wait_send()
 
 
 def partial_scratch(chans, window, pixels, planes, groups, size):
@@ -253,14 +289,20 @@
 
 def exchange_scratch(views, size, pixels):
     width = pixels + 2 * COLS
+    rows = views // 2
     return [
-        pltpu.VMEM((views - 1, size, width), jnp.float32),
+        pltpu.VMEM((rows, size, width), jnp.float32),
+        pltpu.VMEM((rows, size, width), jnp.float32),
+        pltpu.VMEM((rows, size, width), jnp.float32),
+        pltpu.VMEM((rows - 1, size, width), jnp.float32),
         pltpu.VMEM((2, size, COLS), jnp.float32),
         pltpu.VMEM((2, size, COLS), jnp.float32),
         pltpu.VMEM((2, pixels), jnp.float32),
         pltpu.VMEM((views - 1, 2, pixels), jnp.float32),
-        pltpu.SemaphoreType.DMA((views - 1,)),
-        pltpu.SemaphoreType.DMA((views - 1,)),
+        pltpu.SemaphoreType.DMA((rows,)),
+        pltpu.SemaphoreType.DMA((rows,)),
+        pltpu.SemaphoreType.DMA((rows - 1,)),
+        pltpu.SemaphoreType.DMA((rows - 1,)),
         pltpu.SemaphoreType.DMA((2,)),
         pltpu.SemaphoreType.DMA((2,)),
         pltpu.SemaphoreType.DMA((views - 1,)),
@@ -276,19 +318,20 @@
     size = planes // views
     groups = conv_weight.shape[3]
     window = src_feat.shape[3]
-    width = pixels + 2 * COLS
     vmem = pl.BlockSpec(memory_space=pltpu.VMEM)
+    anywhere = pl.BlockSpec(memory_space=pl.ANY)
     inputs = (taps.reshape(planes), ref_feat, src_feat, weights, conv_weight)
-    in_specs = [pl.BlockSpec(memory_space=pltpu.SMEM), vmem, vmem, vmem, vmem]
+    in_specs = [pl.BlockSpec(memory_space=pltpu.SMEM), anywhere, anywhere, anywhere, vmem]
     outs = (jax.ShapeDtypeStruct((size, pixels), jnp.float32), jax.ShapeDtypeStruct((1, pixels), jnp.float32))
+    fetched = [pltpu.VMEM(x.shape, x.dtype) for x in (ref_feat, src_feat, weights)] + [pltpu.SemaphoreType.DMA((3,))]
     local = partial_scratch(chans, window, pixels, planes, groups, size)
     log_prob, depth_map = pl.pallas_call(
         functools.partial(whole_kernel, size, groups, views, tiles),
         out_shape=outs,
         in_specs=in_specs,
         out_specs=(vmem, vmem),
-        scratch_shapes=local + [pltpu.VMEM((views, size, width), jnp.float32)] + exchange_scratch(views, size, pixels),
-        compiler_params=pltpu.CompilerParams(collective_id=0, has_side_effects=True, vmem_limit_bytes=48 * 1024 * 1024),
+        scratch_shapes=fetched + local + exchange_scratch(views, size, pixels),
+        compiler_params=pltpu.CompilerParams(collective_id=0, has_side_effects=True, vmem_limit_bytes=56 * 1024 * 1024),
     )(*inputs)
     return log_prob, depth_map[0]
 

time: 58.6 us -> 51.9 us (0.89)
  local copies, waits for them, and re-layouts: 6.12 us -> 2.86 us
  Pallas kernels: 51 us -> 48.1 us
    unnamed x12 -> x2, local copies, waits for them, and re-layouts: 6.12 us -> 2.86 us
    pallas_call x1, Pallas kernels: 51 us -> 48.1 us  [on_device(): pl.pallas_call(functools.partial(whole_kernel, size, groups, views, tiles...]
where the time goes in v4:
time: 51.9 us; the launch traced here: 51.6 us
  Pallas kernels  48.1 us (93%)
  local copies, waits for them, and re-layouts  2.86 us (6%)
  between operations  0.64 us (1%)
    pallas_call x1, Pallas kernels, on_device(): pl.pallas_call(functools.partial(whole_kernel, size, groups, views, tiles...  48.1 us
    unnamed x2, local copies, waits for them, and re-layouts  2.86 us

profile of v4, /device:TPU:0, one launch (start us, length us, event | category | flops | bytes accessed | tf_op | source)
XLA Modules:
  0.0 51.6 jit_solution(16157320587579307482)
XLA Ops:
  0.6 48.1 %shard_map.68 = (f32[16,2048]{1,0:T(8,128)}, f32[1,2048]{1,0:T(1,128)}) custom-call(s32[128]{0:T(128)} %bitcast.3, bf16[32,2048]{1,0:T(8,128)(2,1)} %ref_hbm.1, bf16[1,1,32,6144]{3,2,1,0:T(8,128)(2,1)} %src_hbm.1, bf16[1,128,4,2048]{3,2,1,0:T(4,128)(2,1)} %weights_hbm.1, f32[3,3,3,8]{3,2,1,0:T(4,128)} %filt_ref.1), custom_call_target="tpu_custom_call" | custom-call | tf_op jit(solution)/shard_map/pallas_call | solution.py:328
  48.7 1.6 %copy.9 = f32[16,2048]{1,0:T(8,128)} copy(f32[16,2048]{1,0:T(8,128)} %get-tuple-element.8) | data formatting | bytes 262144
  50.3 1.3 %copy.10 = f32[2048]{0:T(1024)} copy(f32[2048]{0:T(1024)} %bitcast.2) | data formatting | bytes 16384

commit v5 on v4

--- a/solution.py
+++ b/solution.py
@@ -59,24 +59,26 @@
         pick = jnp.where(shift[...] == rest, jnp.bfloat16(1), jnp.bfloat16(0))
         cut = win[pl.ds(offset >> 7, tiles + step)].reshape((tiles + step) * chans, 2 * LANES)
         moved.append(dot32(cut, pick))
+
+    def tap_row(k, tap, t):
+        row = jnp.broadcast_to(wbuf[k, tap : tap + 1, t * LANES : (t + 1) * LANES], (groups, LANES))
+        return jnp.concatenate([row] * (chans // groups), axis=0)
+
     results = []
     for k in range(2):
-        out = []
-        for i in range(tiles):
-            lanes = slice(i * LANES, (i + 1) * LANES)
-            near = moved[k][i * chans : (i + 1) * chans]
-            far = moved[k][(i + step) * chans : (i + step + 1) * chans]
-            taps4 = (near[:, :LANES], near[:, LANES:], far[:, :LANES], far[:, LANES:])
-            warped = None
-            for tap in range(4):
-                row = jnp.broadcast_to(wbuf[k, tap : tap + 1, lanes], (groups, LANES))
-                row = jnp.concatenate([row] * (chans // groups), axis=0)
-                warped = row * taps4[tap] if warped is None else warped + row * taps4[tap]
-            product = warped * ref_f[i]
-            total = product[:groups]
-            for c in range(1, chans // groups):
-                total = total + product[c * groups : (c + 1) * groups]
-            out.append(total)
+        out, near = [], []
+        for t in range(tiles + step):
+            here = moved[k][t * chans : (t + 1) * chans]
+            sides = (here[:, :LANES], here[:, LANES:])
+            if t >= step:
+                warped = near[t - step] + tap_row(k, 2, t - step) * sides[0] + tap_row(k, 3, t - step) * sides[1]
+                product = warped * ref_f[t - step]
+                total = product[:groups]
+                for c in range(1, chans // groups):
+                    total = total + product[c * groups : (c + 1) * groups]
+                out.append(total)
+            if t < tiles:
+                near.append(tap_row(k, 0, t) * sides[0] + tap_row(k, 1, t) * sides[1])
         results.append(out)
     start = pl.multiple_of((pair + 1) * 2 * groups, 2 * groups)
     for i in range(tiles):
@@ -85,12 +87,14 @@
         clo[pl.ds(start, 2 * groups), i * LANES : (i + 1) * LANES] = lo
 
 
-def filter_slab(slab, size, groups, whi, wlo, chi, clo):
+def filter_slab(slab, size, groups, wboth, chi, clo):
     pixels = chi.shape[1]
     start = pl.multiple_of(slab * size * groups, 2 * groups)
     high = chi[pl.ds(start, (size + 4) * groups), :]
     low = clo[pl.ds(start, (size + 4) * groups), :]
-    part = dot32(whi[...], high) + dot32(whi[...], low) + dot32(wlo[...], high)
+    both = dot32(wboth[...], high)
+    taps9 = 9 * size
+    part = both[:taps9] + both[taps9:] + dot32(wboth[:taps9], low)
     zeros = jnp.zeros((size, COLS), jnp.float32)
     width = pixels + 2 * COLS
     col = lax.broadcasted_iota(jnp.int32, (size, width), 1) & (COLS - 1)
@@ -108,9 +112,9 @@
     return shifted[1] + left + right
 
 
-def filter_matrix(filt_ref, whi, wlo, groups):
-    cols = whi.shape[1]
-    size = whi.shape[0] // 9
+def filter_matrix(filt_ref, wboth, groups):
+    cols = wboth.shape[1]
+    size = wboth.shape[0] // 18
     group = lax.broadcasted_iota(jnp.int32, (groups, cols), 0)
     spread = ((lax.broadcasted_iota(jnp.int32, (groups, cols), 1) & (groups - 1)) == group)
     spread = spread.astype(jnp.float32).astype(jnp.bfloat16)
@@ -119,12 +123,12 @@
     for b in range(3):
         over = [[dot32(part, spread) for part in split_bf16(filt_ref[a, b])] for a in range(3)]
         for e in range(3):
-            at = (b * 3 + e) * size
-            for out, which in ((whi, 0), (wlo, 1)):
+            for which in range(2):
                 total = jnp.zeros((size, cols), jnp.float32)
                 for a in range(3):
                     total = jnp.where(apart == a + 1, over[a][which][e : e + 1], total)
-                out[at : at + size] = total.astype(jnp.bfloat16)
+                at = ((which * 3 + b) * 3 + e) * size
+                wboth[at : at + size] = total.astype(jnp.bfloat16)
 
 
 def peer_at(view, tile):
@@ -194,9 +198,9 @@
         device_id=peer_at(lax.rem(view + 2 + 2 * i, views), tile), device_id_type=MESH)
 
 
-def prepare(taps_ref, ref_ref, src_ref, filt_ref, stage, win, ref_f, shift, chi, clo, whi, wlo, groups):
+def prepare(taps_ref, ref_ref, src_ref, filt_ref, stage, win, ref_f, shift, chi, clo, wboth, groups):
     load_features(src_ref, ref_ref, stage, win, ref_f, shift, groups)
-    filter_matrix(filt_ref, whi, wlo, groups)
+    filter_matrix(filt_ref, wboth, groups)
     edge = jnp.zeros((2 * groups, chi.shape[1]), jnp.bfloat16)
     for buf in (chi, clo):
         buf[: 2 * groups] = edge
@@ -205,7 +209,7 @@
 
 def whole_kernel(size, groups, views, tiles, taps_ref, ref_hbm, src_hbm, weights_hbm, filt_ref, prob_ref, depth_ref,
                  ref_ref, src_ref, weights_ref, load_sem,
-                 stage, win, ref_f, shift, wbuf, chi, clo, whi, wlo, zside, zown,
+                 stage, win, ref_f, shift, wbuf, chi, clo, wboth, zside, zown,
                  xin, zin, hout, hin, sout, sin, xsend, xrecv, zsend, zrecv, hsend, hrecv, ssend, srecv):
     loads = [
         pltpu.make_async_copy(source, target, load_sem.at[n])
@@ -218,7 +222,7 @@
     greet_peers(views, tiles, barrier)
     loads[0].wait()
     loads[1].wait()
-    prepare(taps_ref, ref_ref, src_ref, filt_ref, stage, win, ref_f, shift, chi, clo, whi, wlo, groups)
+    prepare(taps_ref, ref_ref, src_ref, filt_ref, stage, win, ref_f, shift, chi, clo, wboth, groups)
     loads[2].wait()
     pl.semaphore_wait(barrier, views + 1)
     view = lax.axis_index("view")
@@ -246,11 +250,11 @@
             pairs_from(origin, 0, 2)
 
         pairs_from(origin, low, high)
-        zside[i] = filter_slab(2 * row + 1 - col, size, groups, whi, wlo, chi, clo)
+        zside[i] = filter_slab(2 * row + 1 - col, size, groups, wboth, chi, clo)
         side_copy(i, zside, xin, xsend, xrecv).start()
         low, high = jnp.where(col == 0, 2, half + 2), jnp.where(col == 0, half, size + final + 1)
         pairs_from(origin, low, high)
-        own = filter_slab(2 * row + col, size, groups, whi, wlo, chi, clo)
+        own = filter_slab(2 * row + col, size, groups, wboth, chi, clo)
         side_copy(i, zside, xin, xsend, xrecv).wait_recv()
         zown[i] = own + xin[i]
 
@@ -282,8 +286,7 @@
         pltpu.VMEM((2, 4, pixels), jnp.float32),
         pltpu.VMEM(((planes + 4) * groups, pixels), jnp.bfloat16),
         pltpu.VMEM(((planes + 4) * groups, pixels), jnp.bfloat16),
-        pltpu.VMEM((9 * size, (size + 4) * groups), jnp.bfloat16),
-        pltpu.VMEM((9 * size, (size + 4) * groups), jnp.bfloat16),
+        pltpu.VMEM((18 * size, (size + 4) * groups), jnp.bfloat16),
     ]
 
 

time: 51.9 us -> 51.8 us (level)
  no operation moved by 1% of the time
where the time goes in v5:
time: 51.8 us; the launch traced here: 51.5 us
  Pallas kernels  48 us (93%)
  local copies, waits for them, and re-layouts  2.86 us (6%)
  between operations  0.64 us (1%)
    pallas_call x1, Pallas kernels, on_device(): pl.pallas_call(functools.partial(whole_kernel, size, groups, views, tiles...  48 us
    unnamed x2, local copies, waits for them, and re-layouts  2.86 us

profile of v5, /device:TPU:0, one launch (start us, length us, event | category | flops | bytes accessed | tf_op | source)
XLA Modules:
  0.0 51.5 jit_solution(13707835469881436766)
XLA Ops:
  0.6 48.0 %shard_map.68 = (f32[16,2048]{1,0:T(8,128)}, f32[1,2048]{1,0:T(1,128)}) custom-call(s32[128]{0:T(128)} %bitcast.3, bf16[32,2048]{1,0:T(8,128)(2,1)} %ref_hbm.1, bf16[1,1,32,6144]{3,2,1,0:T(8,128)(2,1)} %src_hbm.1, bf16[1,128,4,2048]{3,2,1,0:T(4,128)(2,1)} %weights_hbm.1, f32[3,3,3,8]{3,2,1,0:T(4,128)} %filt_ref.1), custom_call_target="tpu_custom_call" | custom-call | tf_op jit(solution)/shard_map/pallas_call | solution.py:331
  48.6 1.6 %copy.9 = f32[16,2048]{1,0:T(8,128)} copy(f32[16,2048]{1,0:T(8,128)} %get-tuple-element.8) | data formatting | bytes 262144
  50.2 1.3 %copy.10 = f32[2048]{0:T(1024)} copy(f32[2048]{0:T(1024)} %bitcast.2) | data formatting | bytes 16384

commit v6 on v5

--- a/solution.py
+++ b/solution.py
@@ -224,7 +224,6 @@
     loads[1].wait()
     prepare(taps_ref, ref_ref, src_ref, filt_ref, stage, win, ref_f, shift, chi, clo, wboth, groups)
     loads[2].wait()
-    pl.semaphore_wait(barrier, views + 1)
     view = lax.axis_index("view")
     col = lax.rem(view, 2)
     rows = views // 2
@@ -251,6 +250,11 @@
 
         pairs_from(origin, low, high)
         zside[i] = filter_slab(2 * row + 1 - col, size, groups, wboth, chi, clo)
+
+        @pl.when(i == 0)
+        def _():
+            pl.semaphore_wait(barrier, views + 1)
+
         side_copy(i, zside, xin, xsend, xrecv).start()
         low, high = jnp.where(col == 0, 2, half + 2), jnp.where(col == 0, half, size + final + 1)
         pairs_from(origin, low, high)

time: 51.8 us -> 51.9 us (level)
  no operation moved by 1% of the time
where the time goes in v6:
time: 51.9 us; the launch traced here: 51.3 us
  Pallas kernels  47.8 us (92%)
  local copies, waits for them, and re-layouts  2.86 us (6%)
  between operations  0.64 us (1%)
    pallas_call x1, Pallas kernels, on_device(): pl.pallas_call(functools.partial(whole_kernel, size, groups, views, tiles...  47.8 us
    unnamed x2, local copies, waits for them, and re-layouts  2.86 us

profile of v6, /device:TPU:0, one launch (start us, length us, event | category | flops | bytes accessed | tf_op | source)
XLA Modules:
  0.0 51.3 jit_solution(8444038906571525858)
XLA Ops:
  0.6 47.8 %shard_map.68 = (f32[16,2048]{1,0:T(8,128)}, f32[1,2048]{1,0:T(1,128)}) custom-call(s32[128]{0:T(128)} %bitcast.3, bf16[32,2048]{1,0:T(8,128)(2,1)} %ref_hbm.1, bf16[1,1,32,6144]{3,2,1,0:T(8,128)(2,1)} %src_hbm.1, bf16[1,128,4,2048]{3,2,1,0:T(4,128)(2,1)} %weights_hbm.1, f32[3,3,3,8]{3,2,1,0:T(4,128)} %filt_ref.1), custom_call_target="tpu_custom_call" | custom-call | tf_op jit(solution)/shard_map/pallas_call | solution.py:335
  48.4 1.6 %copy.9 = f32[16,2048]{1,0:T(8,128)} copy(f32[16,2048]{1,0:T(8,128)} %get-tuple-element.8) | data formatting | bytes 262144
  50.0 1.3 %copy.10 = f32[2048]{0:T(1024)} copy(f32[2048]{0:T(1024)} %bitcast.2) | data formatting | bytes 16384
